TPU v7x, 256 devices: a whole 4x4x8 slice. The times are simulated.
256 devices in a mesh: seq: 16 (over x, y), vocab: 16 (over z, core).
Axes of the slice: x: 4, y: 4, z: 8, core: 2. Of those that a mesh axis runs over, the one named last changes fastest.
Arguments:
- hidden: bfloat16 [16, 2048, 4608], P('seq', None, 'vocab'), may hold values from -60 to 60
- picks: int32 [16, 64], P('seq'), may hold values from 0 to 2047
- counts: int32 [16], P('seq'), may hold values from 1 to 64, 512 in all
- norm_gain: float32 [4608], P('vocab'), may hold values from 0.5 to 1.5
- head_weight: bfloat16 [196608, 4608], P(('vocab', 'seq')), may hold values from -3 to 3
Outputs:
- log_probs: float32 [1024, 196608], P('seq', 'vocab')
Inputs may be any that keep to these rules, and one draw needn't show every extreme that they name: The counts sum to exactly 512, and the largest is exactly 64.
All inputs are finite; a program needn't handle non-finite values. No bound on the sum of `counts` on one device may be relied on, other than what follows from the above.
Results may differ from a plain program's by a relative error of at most 0.00034.
Values may be sent and summed in bfloat16 or wider, within the bound.
A program may use at most 64 MiB of HBM per device.

v0:
```python
import jax
import jax.numpy as jnp
from jax import lax
from jax.sharding import PartitionSpec as P

SOFT_CAP = 30.0
EPSILON = 1e-06


def soft_capped(values):
    return SOFT_CAP * jnp.tanh(values / SOFT_CAP)


def local(hidden, picks, counts, norm_gain, head_weight):
    slot_count = picks.shape[1]
    model_width = head_weight.shape[1]
    selected = jnp.take(hidden[0], picks[0], axis=0).astype(jnp.float32)
    partial_value = jnp.sum(selected * selected, axis=1)
    square_total = lax.psum(partial_value, "vocab")
    inverse_rms = lax.rsqrt(square_total / model_width + EPSILON)
    normed_cols = (selected * inverse_rms[:, None] * norm_gain[None, :]).astype(jnp.bfloat16)
    normed = lax.all_gather(normed_cols, "vocab", axis=1, tiled=True)
    capped = soft_capped(
        jnp.einsum(
            "rd,vd->rv",
            lax.all_gather(normed, "seq", axis=0, tiled=True),
            head_weight,
            preferred_element_type=jnp.float32,
        )
    )
    partition = lax.psum(jnp.sum(jnp.exp(capped), axis=1), ("seq", "vocab"))
    log_rows = capped - jnp.log(partition)[:, None]
    owned_rows = lax.all_to_all(log_rows, "seq", split_axis=0, concat_axis=1, tiled=True)
    live_mask = lax.iota(jnp.int32, slot_count) < counts[0]
    return jnp.where(live_mask[:, None], owned_rows, jnp.zeros_like(owned_rows))


def solution(mesh):
    in_specs = (
        P("seq", None, "vocab"),
        P("seq", None),
        P("seq"),
        P("vocab"),
        P(("vocab", "seq"), None),
    )
    out_specs = P("seq", "vocab")
    return jax.shard_map(local, mesh=mesh, in_specs=in_specs, out_specs=out_specs, check_vma=False)
```

profile of v0, /device:TPU:1, one launch (start us, length us, event | category | flops | bytes accessed | tf_op | source)
XLA Modules:
  0.0 281.9 jit_solution(10943737605370799342)
XLA Ops:
  6.5 0.0 copy-start
  6.5 0.0 all-gather.3.cloned.1.call-start
  6.5 0.7 fusion.5
  7.2 0.7 compare_and_fusion
  7.9 1.8 copy.11
  9.7 0.7 gather_fusion
  10.4 0.2 fusion.1
  10.6 27.4 %psum.14 = f32[64]{0:T(128)S(1)} all-reduce(f32[64]{0:T(128)S(1)} %fusion.1), channel_id=1, replica_groups=mesh['seq'=16,'vocab'=16] {'vocab'}, use_global_device_ids=true, to_apply=%region_1.2 | all-reduce | flops 64 | bytes 512 | tf_op jit(solution)/shard_map/psum | solution.py:19
  38.0 0.0 copy-done
  38.0 0.1 fusion.4
  38.1 19.4 %all-gather = bf16[16,288,64]{1,2,0:T(8,128)(2,1)S(1)} all-gather(bf16[1,288,64]{1,2,0:T(8,128)(2,1)S(1)} %fusion.4), channel_id=1, replica_groups=mesh['seq'=16,'vocab'=16] {'vocab'}, dimensions={0}, use_global_device_ids=true | all-gather | bytes 626688 | tf_op jit(solution)/shard_map/all_gather | solution.py:22
  57.5 0.5 copy.12
  58.0 1.6 reshape.53
  59.6 0.0 all-gather.3.cloned.1.call-update
  59.6 78.3 %all-gather.3.cloned.1.call-done = bf16[1024,4608]{1,0:T(8,128)(2,1)} async-done(((bf16[64,4608]{1,0:T(8,128)(2,1)}), bf16[1024,4608]{1,0:T(8,128)(2,1)}) %all-gather.3.cloned.1.call-update) | async-done | bytes 9437200 | tf_op jit(solution)/shard_map/all_gather | solution.py:26
  137.9 12.6 %exponential_reduce_fusion = (f32[1024]{0:T(1024)S(1)}, f32[1024,768]{1,0:T(8,128)S(1)}) fusion(bf16[1024,4608]{1,0:T(8,128)(2,1)} %all-gather.3.cloned.1.call-done, bf16[768,4608]{1,0:T(8,128)(2,1)} %param.9), kind=kOutput, calls=%fused_computation.1 | convolution fusion | flops 7250115584 | bytes 19664896 | tf_op jit(solution)/shard_map/rd,vd->rv/dot_general | solution.py:24
  150.5 76.0 %psum.15 = f32[1024]{0:T(1024)S(1)} all-reduce(f32[1024]{0:T(1024)S(1)} %get-tuple-element.5), channel_id=1, replica_groups=mesh['seq'=16,'vocab'=16] {'seq','vocab'}, use_global_device_ids=true, to_apply=%region_3.4 | all-reduce | flops 1024 | bytes 8192 | tf_op jit(solution)/shard_map/psum | solution.py:31
  226.5 2.1 fusion
  228.6 3.7 %all-to-all-start = ((f32[16,64,768]{2,1,0:T(8,128)}), f32[16,64,768]{2,1,0:T(8,128)S(1)}, u32[]{:S(2)}, u32[]{:S(2)}) async-start(f32[16,64,768]{2,1,0:T(8,128)} %bitcast.24), calls=%async_computation | async-start | bytes 6291456 | tf_op jit(solution)/shard_map/all_to_all | solution.py:33
  233.1 39.7 %all-to-all-done = f32[16,64,768]{2,1,0:T(8,128)S(1)} async-done(((f32[16,64,768]{2,1,0:T(8,128)}), f32[16,64,768]{2,1,0:T(8,128)S(1)}, u32[]{:S(2)}, u32[]{:S(2)}) %all-to-all-start) | async-done | bytes 3145760 | tf_op jit(solution)/shard_map/all_to_all | solution.py:33
  272.8 0.3 copy.14
  273.1 2.0 broadcast_select_fusion
  (4 shorter events, 0.0 us)
Async XLA Ops:
  6.5 31.5 %copy-start = (f32[288]{0:T(512)S(1)}, f32[288]{0:T(512)}, u32[]{:S(2)}) copy-start(f32[288]{0:T(512)} %param.8) | copy-start | bytes 3460
  6.5 131.4 %all-gather.3.cloned.1.call-start = ((), (), s32[]{:S(2)}) async-start(), calls=%async_computation.1 | async-start | bytes 10027008 | tf_op jit(solution)/shard_map/all_gather | solution.py:26
  228.6 44.1 %all-to-all-start = ((f32[16,64,768]{2,1,0:T(8,128)}), f32[16,64,768]{2,1,0:T(8,128)S(1)}, u32[]{:S(2)}, u32[]{:S(2)}) async-start(f32[16,64,768]{2,1,0:T(8,128)} %bitcast.24), calls=%async_computation | async-start | bytes 6291456 | tf_op jit(solution)/shard_map/all_to_all | solution.py:33
Sparse Core Ops, SparseCore 0:
  59.7 78.1 all-gather.2
where the time goes:
time: 286 us; the launch traced here: 282 us
  blocking collectives  123 us (43%)
  waiting for transfers between devices  118 us (41%)
  between operations  14.1 us (5%)
  matrix products  12.6 us (4%)
  other arithmetic  5.74 us (2%)
  local copies, waits for them, and re-layouts  4.9 us (2%)
  starting transfers between devices  3.74 us (1%)
    all_gather x1, waiting for transfers between devices, local(): lax.all_gather(normed, 'seq', axis=0, tiled=True)  78.3 us
    psum x1, blocking collectives, local(): partition = lax.psum(jnp.sum(jnp.exp(capped), axis=1), ('seq', 'vocab'))  76 us
    all_to_all x1, waiting for transfers between devices, local(): lax.all_to_all(log_rows, 'seq', split_axis=0, concat_axis=1, tiled=True)  39.7 us
    psum x1, blocking collectives, local(): square_total = lax.psum(partial_value, 'vocab')  27.4 us
    all_gather x1, blocking collectives, local(): normed = lax.all_gather(normed_cols, 'vocab', axis=1, tiled=True)  19.4 us
    dot_general x1, matrix products, local(): jnp.einsum('rd,vd->rv', lax.all_gather(normed, 'seq', axis=0, tiled=True)...  12.6 us
  transfers between devices with their start and end apart: 2, of which 2 were waited for; matrix products, arithmetic and copies ran while one was open for 0% of the time, Pallas kernels for 0%

commit v1 on v0

v1 whole, which is shorter than its diff:
```python
import functools

import jax
import jax.numpy as jnp
from jax import lax
from jax.experimental import pallas as pl
from jax.experimental.pallas import tpu as pltpu
from jax.sharding import PartitionSpec as P

SOFT_CAP = 30.0
EPSILON = 1e-06
CODE = 32767.0
HALF = 16
MESH = pl.DeviceIdType.MESH


def iota(shape, dim):
    return lax.broadcasted_iota(jnp.int32, shape, dim)


def kernel(
    dims,
    hidden_ref,
    picks_ref,
    counts_ref,
    gain_ref,
    head_ref,
    codes_ref,
    logs_ref,
    head,
    cnt,
    sqs,
    place,
    placed,
    feats,
    rows_x,
    level,
    expo,
    send,
    sums_a,
    sums_b,
    head_sem,
    own_sem,
    cnt_s, cnt_r,
    sqs_s, sqs_r,
    plc_s, plc_r,
    fea_s, fea_r,
    sib_s, sib_r,
    one_s, one_r,
    two_s, two_r,
    fwd_s, fwd_r,
    out_s, out_r,
    sma_s, sma_r,
    smb_s, smb_r,
):
    n_seq, n_vocab, side, slots, total = dims
    rows = total // n_seq
    width = head_ref.shape[1]
    entries = head_ref.shape[0]
    features = hidden_ref.shape[0]
    half_width = width // 2
    n_z = n_vocab // 2
    s = lax.axis_index("seq")
    v = lax.axis_index("vocab")
    x, y = s // side, s % side
    z, core = v // 2, v % 2
    sibling = 2 * z + (1 - core)

    def seq_peer(p):
        return (s + p) % n_seq

    def vocab_peer(p):
        return (v + p) % n_vocab

    load_head = pltpu.make_async_copy(head_ref, head, head_sem)
    load_head.start()

    barrier = pltpu.get_barrier_semaphore()

    def greet_seq(p, c):
        pl.semaphore_signal(barrier, inc=1, device_id={"seq": seq_peer(p)}, device_id_type=MESH)
        return c

    def greet_vocab(p, c):
        pl.semaphore_signal(barrier, inc=1, device_id={"vocab": vocab_peer(p)}, device_id_type=MESH)
        return c

    lax.fori_loop(1, n_seq, greet_seq, 0)
    lax.fori_loop(1, n_vocab, greet_vocab, 0)
    pl.semaphore_wait(barrier, n_seq + n_vocab - 2)

    def exchange(count, axis, peer, src, dst, send_sem, recv_sem):
        def copy(p):
            return pltpu.make_async_remote_copy(
                src_ref=src(p), dst_ref=dst, send_sem=send_sem.at[p], recv_sem=recv_sem.at[p],
                device_id={axis: peer(p)}, device_id_type=MESH,
            )

        def begin(p, c):
            copy(p).start()
            return c

        def wait_recv(p, c):
            copy(p).wait_recv()
            return c

        def wait_send(p, c):
            copy(p).wait_send()
            return c

        def start():
            lax.fori_loop(1, count, begin, 0)

        def received():
            lax.fori_loop(1, count, wait_recv, 0)

        def sent():
            lax.fori_loop(1, count, wait_send, 0)

        return start, received, sent

    cnt[pl.ds(s, 1)] = jnp.full((1, 8, 128), counts_ref[0], jnp.int32)
    cnt_start, cnt_received, cnt_sent = exchange(
        n_seq, "seq", seq_peer, lambda p: cnt.at[s], cnt.at[s], cnt_s, cnt_r
    )
    cnt_start()

    one_hot = (iota((hidden_ref.shape[1], slots), 0) == picks_ref[...]).astype(jnp.bfloat16)
    selected = jnp.dot(hidden_ref[...], one_hot, preferred_element_type=jnp.float32)
    square = jnp.sum(selected * selected, axis=0, keepdims=True)
    square = jnp.concatenate([square, jnp.zeros((1, 128 - slots), jnp.float32)], axis=1)
    sqs[pl.ds(v, 1)] = jnp.broadcast_to(square, (8, 128))[None]
    sqs_start, sqs_received, sqs_sent = exchange(
        n_vocab, "vocab", vocab_peer, lambda p: sqs.at[v], sqs.at[v], sqs_s, sqs_r
    )
    sqs_start()
    diagonal = iota((features, features), 0) == iota((features, features), 1)
    gain = jnp.sum(jnp.where(diagonal, gain_ref[...], 0.0), axis=1, keepdims=True)

    cnt_received()
    group = iota((n_seq, 8, 128), 0)
    every = cnt[...]
    offset = jnp.sum(jnp.where(group < s, every, 0), axis=0)[0:1, 0:1]
    count = jnp.sum(jnp.where(group == s, every, 0), axis=0)[0:1, 0:1]

    slot = iota((total, slots), 1)
    placing = ((iota((total, slots), 0) == offset + slot) & (slot < count)).astype(jnp.bfloat16)

    sqs_received()
    mean_square = jnp.sum(sqs[...], axis=0)[0:1, 0:slots] / width
    normed = (selected * lax.rsqrt(mean_square + EPSILON) * gain).astype(jnp.bfloat16)

    compact = lax.dot_general(
        placing, normed, (((1,), (1,)), ((), ())), preferred_element_type=jnp.float32
    ).astype(jnp.bfloat16)
    place[...] = compact.reshape(n_seq, rows, features)
    plc_start, plc_received, plc_sent = exchange(
        n_seq, "seq", seq_peer, lambda p: place.at[seq_peer(p)], placed.at[s], plc_s, plc_r
    )
    plc_start()
    placed[pl.ds(s, 1)] = place[pl.ds(s, 1)]
    plc_received()
    block = jnp.sum(placed[...].astype(jnp.float32), axis=0).astype(jnp.bfloat16)

    feats[pl.ds(v, 1)] = block[None]

    def z_peer(p):
        return 2 * ((z + p) % n_z) + core

    fea_start, fea_received, fea_sent = exchange(
        n_z, "vocab", z_peer, lambda p: feats.at[v], feats.at[v], fea_s, fea_r
    )
    fea_start()

    def hand_over(p):
        of = 2 * ((z + n_z - p) % n_z) + core
        return pltpu.make_async_remote_copy(
            src_ref=feats.at[of], dst_ref=feats.at[of], send_sem=sib_s.at[p], recv_sem=sib_r.at[p],
            device_id={"vocab": sibling}, device_id_type=MESH,
        )

    hand_over(0).start()

    def pass_on(p, c):
        pltpu.make_async_remote_copy(
            src_ref=feats.at[v], dst_ref=feats.at[v], send_sem=fea_s.at[p], recv_sem=fea_r.at[p],
            device_id={"vocab": z_peer(p)}, device_id_type=MESH,
        ).wait_recv()
        hand_over(p).start()
        return c

    def handed(p, c):
        hand_over(p).wait_recv()
        return c

    def handed_off(p, c):
        hand_over(p).wait_send()
        return c

    lax.fori_loop(1, n_z, pass_on, 0)
    lax.fori_loop(0, n_z, handed, 0)
    own = jnp.concatenate([feats[i] for i in range(n_vocab)], axis=1)
    for k in range(2):
        part = own[:, k * half_width : (k + 1) * half_width]
        rows_x[0, k, 0, pl.ds(x, 1)] = part[:HALF][None]
        rows_x[0, k, 1, pl.ds(y, 1)] = part[HALF:][None]

    def across(order, p):
        if order == 0:
            return ((x + p) % side) * side + y
        return x * side + (y + p) % side

    def spot(order, j):
        return ((x if order == 0 else y) + side - j) % side

    def first(order, p):
        at = rows_x.at[0, core, order, spot(order, 0)]
        return pltpu.make_async_remote_copy(
            src_ref=at, dst_ref=at, send_sem=one_s.at[order, p], recv_sem=one_r.at[order, p],
            device_id={"seq": across(order, p)}, device_id_type=MESH,
        )

    def second(order, p, j):
        return pltpu.make_async_remote_copy(
            src_ref=rows_x.at[0, core, order, spot(order, j)],
            dst_ref=rows_x.at[p, core, order, spot(order, j)],
            send_sem=two_s.at[order, p, j], recv_sem=two_r.at[order, p, j],
            device_id={"seq": across(1 - order, p)}, device_id_type=MESH,
        )

    def over(kind, order, p, j):
        at = rows_x.at[p, kind, order, spot(order, j)]
        return pltpu.make_async_remote_copy(
            src_ref=at, dst_ref=at, send_sem=fwd_s.at[order, p, j], recv_sem=fwd_r.at[order, p, j],
            device_id={"vocab": sibling}, device_id_type=MESH,
        )

    near = [p for d in range(1, side // 2 + 1) for p in sorted({d, side - d})]
    for p in near:
        for order in range(2):
            first(order, p).start()
    for p in near:
        for order in range(2):
            second(order, p, 0).start()
    for j in near:
        for order in range(2):
            first(order, j).wait_recv()
            for p in near:
                second(order, p, j).start()
            over(core, order, 0, j).start()

    load_head.wait()
    level[pl.ds(total, slots)] = jnp.zeros((slots, entries), jnp.int32)
    columns = 256 if entries % 256 == 0 else entries

    def multiply(p):
        def some(i, total_exp):
            at = pl.ds(pl.multiple_of(i * columns, columns), columns)
            logits = jnp.zeros((2 * side * HALF, columns), jnp.float32)
            for k in range(2):
                logits += lax.dot_general(
                    rows_x[p, k].reshape(2 * side * HALF, half_width),
                    head[at, k * half_width : (k + 1) * half_width],
                    (((1,), (1,)), ((), ())),
                    preferred_element_type=jnp.float32,
                )
            bent = jnp.tanh(logits / SOFT_CAP)
            code = jnp.round(bent * CODE).astype(jnp.int32)
            for order in range(2):
                for piece in range(side):
                    low = (order * side + piece) * HALF
                    level[pl.ds(pl.multiple_of(row_of(p, order, piece), HALF), HALF), at] = code[low : low + HALF]
            e = jnp.exp(SOFT_CAP * bent)
            for c in range(0, columns, 128):
                total_exp += e[:, c : c + 128]
            return total_exp

        total_exp = lax.fori_loop(
            0, entries // columns, some, jnp.zeros((2 * side * HALF, 128), jnp.float32)
        )
        summed = jnp.broadcast_to(jnp.sum(total_exp, axis=1, keepdims=True), total_exp.shape)
        for order in range(2):
            for piece in range(side):
                low = (order * side + piece) * HALF
                expo[pl.ds(pl.multiple_of(row_of(p, order, piece), HALF), HALF)] = summed[low : low + HALF]

    def row_of(p, order, piece):
        if order == 0:
            return (piece * side + (y + side - p) % side) * rows
        return (((x + side - p) % side) * side + piece) * rows + HALF

    for j in near:
        for order in range(2):
            over(1 - core, order, 0, j).wait_recv()
    multiply(0)
    for p in near:
        for j in [0] + near:
            for order in range(2):
                second(order, p, j).wait_recv()
                over(core, order, p, j).start()
        for j in [0] + near:
            for order in range(2):
                over(1 - core, order, p, j).wait_recv()
        multiply(p)

    square_eye = iota((128, 128), 0) == iota((128, 128), 1)
    lines = [
        jnp.sum(jnp.where(square_eye, expo[i * 128 : (i + 1) * 128], 0.0), axis=0, keepdims=True)
        for i in range(total // 128)
    ]
    lines.append(jnp.zeros((8 - len(lines), 128), jnp.float32))
    sums_a[pl.ds(s, 1)] = jnp.concatenate(lines, axis=0)[None]
    sma_start, sma_received, sma_sent = exchange(
        n_seq, "seq", seq_peer, lambda p: sums_a.at[s], sums_a.at[s], sma_s, sma_r
    )
    sma_start()


    def result(p):
        return pltpu.make_async_remote_copy(
            src_ref=send.at[p], dst_ref=codes_ref.at[s], send_sem=out_s.at[p], recv_sem=out_r.at[p],
            device_id={"seq": seq_peer(p)}, device_id_type=MESH,
        )

    def fill(p):
        start = jnp.sum(jnp.where(group < seq_peer(p), cnt[...], 0), axis=0)[0:1, 0:1]
        for c in range(0, entries, 128):
            window = level[:, c : c + 128]
            bit = 1 << (total.bit_length() - 2)
            while bit:
                left = bit - 1 + slots if bit > 8 else slots + 8
                left = (left + 7) // 8 * 8
                if bit >= 8:
                    window = jnp.where(start & bit != 0, window[bit : bit + left], window[:left])
                else:
                    window = jnp.where(start & bit != 0, pltpu.roll(window, left - bit, axis=0), window)
                bit //= 2
            send[pl.ds(p, 1), :, c : c + 128] = window[:slots].astype(jnp.int16)[None]

    def give(p, c):
        fill(p)
        result(p).start()
        return c

    lax.fori_loop(1, n_seq, give, 0)
    fill(0)
    keep = pltpu.make_async_copy(send.at[0], codes_ref.at[s], own_sem)
    keep.start()

    sma_received()
    sums_b[pl.ds(v, 1)] = jnp.sum(sums_a[...], axis=0)[None]
    smb_start, smb_received, smb_sent = exchange(
        n_vocab, "vocab", vocab_peer, lambda p: sums_b.at[v], sums_b.at[v], smb_s, smb_r
    )
    smb_start()
    smb_received()
    partition = jnp.sum(sums_b[...], axis=0)
    mine = jnp.zeros((slots, 1), jnp.float32)
    for i in range(total // 128):
        hit = iota((slots, 128), 1) + 128 * i == offset + iota((slots, 128), 0)
        mine += jnp.sum(jnp.where(hit, partition[i : i + 1], 0.0), axis=1, keepdims=True)
    logs_ref[...] = jnp.broadcast_to(jnp.log(jnp.where(mine > 0.0, mine, 1.0)), logs_ref.shape)

    cnt_sent()
    sqs_sent()
    plc_sent()
    fea_sent()
    lax.fori_loop(0, n_z, handed_off, 0)
    for order in range(2):
        for p in near:
            first(order, p).wait_send()
        for j in near:
            over(core, order, 0, j).wait_send()
        for p in near:
            for j in [0] + near:
                second(order, p, j).wait_send()
                over(core, order, p, j).wait_send()
    sma_sent()
    smb_sent()
    keep.wait()

    def got(p, c):
        result(p).wait()
        return c

    lax.fori_loop(1, n_seq, got, 0)


def solution(mesh):
    n_seq, n_vocab = mesh.shape["seq"], mesh.shape["vocab"]
    side = int(round(n_seq**0.5))

    def local(hidden, picks, counts, norm_gain, head_weight):
        slots = picks.shape[1]
        entries, width = head_weight.shape
        features = hidden.shape[2]
        total = n_seq * slots // 2
        rows = total // n_seq
        dma = lambda *shape: [pltpu.SemaphoreType.DMA(shape)] * 2
        vmem = pl.BlockSpec(memory_space=pltpu.VMEM)
        hbm = pl.BlockSpec(memory_space=pl.ANY)
        codes, logs = pl.pallas_call(
            functools.partial(kernel, (n_seq, n_vocab, side, slots, total)),
            out_shape=(
                jax.ShapeDtypeStruct((n_seq, slots, entries), jnp.int16),
                jax.ShapeDtypeStruct((slots, 128), jnp.float32),
            ),
            in_specs=[vmem, vmem, pl.BlockSpec(memory_space=pltpu.SMEM), vmem, hbm],
            out_specs=(hbm, vmem),
            scratch_shapes=[
                pltpu.VMEM((entries, width), jnp.bfloat16),
                pltpu.VMEM((n_seq, 8, 128), jnp.int32),
                pltpu.VMEM((n_vocab, 8, 128), jnp.float32),
                pltpu.VMEM((n_seq, rows, features), jnp.bfloat16),
                pltpu.VMEM((n_seq, rows, features), jnp.bfloat16),
                pltpu.VMEM((n_vocab, rows, features), jnp.bfloat16),
                pltpu.VMEM((side, 2, 2, side, HALF, width // 2), jnp.bfloat16),
                pltpu.VMEM((total + slots, entries), jnp.int32),
                pltpu.VMEM((total, 128), jnp.float32),
                pltpu.VMEM((n_seq, slots, entries), jnp.int16),
                pltpu.VMEM((n_seq, 8, 128), jnp.float32),
                pltpu.VMEM((n_vocab, 8, 128), jnp.float32),
                pltpu.SemaphoreType.DMA,
                pltpu.SemaphoreType.DMA,
                *dma(n_seq),
                *dma(n_vocab),
                *dma(n_seq),
                *dma(n_vocab // 2),
                *dma(n_vocab // 2),
                *dma(2, side),
                *dma(2, side, side),
                *dma(2, side, side),
                *dma(n_seq),
                *dma(n_seq),
                *dma(n_vocab),
            ],
            compiler_params=pltpu.CompilerParams(
                collective_id=0, has_side_effects=True, vmem_limit_bytes=48 << 20
            ),
            cost_estimate=pl.CostEstimate(
                flops=2 * total * entries * width, bytes_accessed=2 * entries * width, transcendentals=2 * total * entries
            ),
        )(jnp.swapaxes(hidden[0], 0, 1), picks, counts, norm_gain[None], head_weight)
        capped = codes.astype(jnp.float32) * (SOFT_CAP / CODE)
        log_rows = jnp.swapaxes(capped, 0, 1).reshape(slots, n_seq * entries) - logs[:, :1]
        live = lax.iota(jnp.int32, slots) < counts[0]
        return jnp.where(live[:, None], log_rows, 0.0)

    in_specs = (
        P("seq", None, "vocab"),
        P("seq", None),
        P("seq"),
        P("vocab"),
        P(("vocab", "seq"), None),
    )
    return jax.shard_map(local, mesh=mesh, in_specs=in_specs, out_specs=P("seq", "vocab"), check_vma=False)
```

time: 286 us -> 100 us (0.35)
  the two profiles are of different devices: /device:TPU:1 before, /device:TPU:60 now
where the time goes in v1:
time: 100 us
  Pallas kernels  93.9 us (94%)
  local copies, waits for them, and re-layouts  3 us (3%)
  other arithmetic  2.56 us (3%)
    pallas_call x1, Pallas kernels, local(): pl.pallas_call(functools.partial(kernel, (n_seq, n_vocab, side, slots, to...  93.9 us

profile of v1, /device:TPU:60, one launch (start us, length us, event | category | flops | bytes accessed | tf_op | source)
XLA Modules:
  0.0 100.1 jit_solution(4536853251136945401)
XLA Ops:
  0.7 0.7 broadcast_in_dim.17.gain_ref
  1.4 0.0 copy-start
  1.4 1.3 %copy-done = bf16[1,2048,288]{1,2,0:T(8,128)(2,1)S(1)} copy-done((bf16[1,2048,288]{1,2,0:T(8,128)(2,1)S(1)}, bf16[1,2048,288]{1,2,0:T(8,128)(2,1)}, u32[]{:S(2)}) %copy-start) | copy-done | bytes 1179672
  2.6 0.0 copy-start.1
  2.6 0.7 copy-done.1
  3.3 93.9 %shard_map.55 = (s16[16,64,768]{2,1,0:T(8,128)(2,1)S(1)}, f32[64,128]{1,0:T(8,128)S(1)}) custom-call(bf16[288,2048]{1,0:T(8,128)(2,1)S(1)} %bitcast.9, s32[1,64]{1,0:T(1,128)S(1)} %copy-done.1, s32[1]{0:T(128)} %copy.8.counts_ref, f32[1,288]{1,0:T(1,128)S(1)} %broadcast_in_dim.17.gain_ref, bf16[768,4608]{1,0:T(8,128)(2,1)} %head_ref.1), custom_call_target="tpu_custom_call" | custom-call | flops 3623878656 | bytes 7077888 | tf_op jit(solution)/shard_map/pallas_call | solution.py:402
  97.2 0.1 slice_reduce_fusion
  97.3 0.6 multiply_bitcast_fusion
  97.8 0.3 copy.7
  98.1 2.0 %subtract_select_fusion = f32[64,12288]{1,0:T(8,128)} fusion(f32[64,12288]{1,0:T(8,128)S(1)} %bitcast.10, f32[64]{0:T(128)S(1)} %slice_reduce_fusion, pred[64]{0:T(512)(128)(4,1)S(1)} %iota_compare_fusion), kind=kLoop, calls=%fused_computation | loop fusion | flops 1572864 | bytes 6291776 | tf_op jit(solution)/shard_map/jit(_where)/select_n | solution.py:447
  (1 shorter events, 0.0 us)
Async XLA Ops:
  1.4 1.3 %copy-start = (bf16[1,2048,288]{1,2,0:T(8,128)(2,1)S(1)}, bf16[1,2048,288]{1,2,0:T(8,128)(2,1)}, u32[]{:S(2)}) copy-start(bf16[1,2048,288]{1,2,0:T(8,128)(2,1)} %param.5) | copy-start | bytes 3538948
  2.6 0.7 copy-start.1

commit v2 on v1

v2 whole, which is shorter than its diff:
```python
import functools

import jax
import jax.numpy as jnp
from jax import lax
from jax.experimental import pallas as pl
from jax.experimental.pallas import tpu as pltpu
from jax.sharding import PartitionSpec as P

SOFT_CAP = 30.0
EPSILON = 1e-06
CODE = 32767.0
HALF = 16
MESH = pl.DeviceIdType.MESH


def iota(shape, dim):
    return lax.broadcasted_iota(jnp.int32, shape, dim)


def kernel(
    dims,
    hidden_ref,
    picks_ref,
    counts_ref,
    gain_ref,
    head_ref,
    codes_ref,
    logs_ref,
    hidden,
    picks,
    gain,
    head,
    cnt,
    gains,
    place,
    placed,
    feats,
    rows_x,
    partial,
    level,
    expo,
    send,
    sums_a,
    sums_b,
    in_sem,
    own_sem,
    cnt_sem,
    gain_sem,
    plc_sem,
    sma_sem,
    smb_sem,
    out_sem,
    fea_s, fea_r,
    sib_s, sib_r,
    one_s, one_r,
    two_s, two_r,
    fwd_s, fwd_r,
):
    n_seq, n_vocab, side, slots, total = dims
    rows = total // n_seq
    width = head_ref.shape[1]
    entries = head_ref.shape[0]
    features = hidden_ref.shape[0]
    block_rows = 2 * side * HALF
    half_width = width // 2
    n_z = n_vocab // 2
    s = lax.axis_index("seq")
    v = lax.axis_index("vocab")
    x, y = s // side, s % side
    z, core = v // 2, v % 2
    sibling = 2 * z + (1 - core)

    def seq_peer(p):
        return (s + p) % n_seq

    def vocab_peer(p):
        return (v + p) % n_vocab

    loads = [
        pltpu.make_async_copy(ref, to, in_sem.at[i])
        for i, (ref, to) in enumerate(
            [(hidden_ref, hidden), (picks_ref, picks), (gain_ref, gain), (head_ref, head)]
        )
    ]
    for load in loads:
        load.start()

    barrier = pltpu.get_barrier_semaphore()

    def greet_seq(p, c):
        pl.semaphore_signal(barrier, inc=1, device_id={"seq": seq_peer(p)}, device_id_type=MESH)
        return c

    def greet_vocab(p, c):
        pl.semaphore_signal(barrier, inc=1, device_id={"vocab": vocab_peer(p)}, device_id_type=MESH)
        return c

    lax.fori_loop(1, n_seq, greet_seq, 0)
    lax.fori_loop(1, n_vocab, greet_vocab, 0)
    pl.semaphore_wait(barrier, n_seq + n_vocab - 2)

    def exchange(count, axis, peer, src, dst, many, sems, prepare=None):
        def copy(p, src, dst):
            return pltpu.make_async_remote_copy(
                src_ref=src, dst_ref=dst, send_sem=sems.at[0], recv_sem=sems.at[1],
                device_id={axis: peer(p)}, device_id_type=MESH,
            )

        def begin(p, c):
            if prepare is not None:
                prepare(p)
            copy(p, src(p), dst).start()
            return c

        def start():
            lax.fori_loop(1, count, begin, 0)

        def received():
            copy(1, many, many).wait_recv()

        def sent():
            copy(1, many, many).wait_send()

        return start, received, sent

    cnt[pl.ds(s, 1)] = jnp.full((1, 8, 128), counts_ref[0], jnp.int32)
    cnt_start, cnt_received, cnt_sent = exchange(
        n_seq, "seq", seq_peer, lambda p: cnt.at[s], cnt.at[s], cnt.at[pl.ds(0, n_seq - 1)], cnt_sem
    )
    cnt_start()

    loads[0].wait()
    loads[1].wait()
    one_hot = (iota((hidden.shape[1], slots), 0) == picks[...]).astype(jnp.bfloat16)
    selected = jnp.dot(hidden[...], one_hot, preferred_element_type=jnp.float32).astype(jnp.bfloat16)

    loads[2].wait()
    gains[pl.ds(v, 1)] = jnp.broadcast_to(gain[...].reshape(1, 1, features), (1, 8, features))
    gain_start, gain_received, gain_sent = exchange(
        n_vocab, "vocab", vocab_peer, lambda p: gains.at[v], gains.at[v], gains.at[pl.ds(0, n_vocab - 1)], gain_sem
    )
    gain_start()

    cnt_received()
    group = iota((n_seq, 8, 128), 0)
    every = cnt[...]
    offset = jnp.sum(jnp.where(group < s, every, 0), axis=0)[0:1, 0:1]
    count = jnp.sum(jnp.where(group == s, every, 0), axis=0)[0:1, 0:1]

    slot = iota((total, slots), 1)
    placing = ((iota((total, slots), 0) == offset + slot) & (slot < count)).astype(jnp.bfloat16)

    compact = lax.dot_general(
        placing, selected, (((1,), (1,)), ((), ())), preferred_element_type=jnp.float32
    ).astype(jnp.bfloat16)
    place[...] = compact.reshape(n_seq, rows, features)
    plc_start, plc_received, plc_sent = exchange(
        n_seq, "seq", seq_peer, lambda p: place.at[seq_peer(p)], placed.at[s], placed.at[pl.ds(0, n_seq - 1)], plc_sem
    )
    plc_start()
    placed[pl.ds(s, 1)] = place[pl.ds(s, 1)]
    plc_received()
    block = jnp.sum(placed[...].astype(jnp.float32), axis=0).astype(jnp.bfloat16)

    feats[pl.ds(v, 1)] = block[None]

    def z_peer(p):
        return 2 * ((z + p) % n_z) + core

    def along(p):
        return pltpu.make_async_remote_copy(
            src_ref=feats.at[v], dst_ref=feats.at[v], send_sem=fea_s.at[p], recv_sem=fea_r.at[p],
            device_id={"vocab": z_peer(p)}, device_id_type=MESH,
        )

    def set_out(p, c):
        along(p).start()
        return c

    def set_off(p, c):
        along(p).wait_send()
        return c

    lax.fori_loop(1, n_z, set_out, 0)

    def hand_over(p):
        of = 2 * ((z + n_z - p) % n_z) + core
        return pltpu.make_async_remote_copy(
            src_ref=feats.at[of], dst_ref=feats.at[of], send_sem=sib_s.at[p], recv_sem=sib_r.at[p],
            device_id={"vocab": sibling}, device_id_type=MESH,
        )

    hand_over(0).start()

    def pass_on(p, c):
        along(p).wait_recv()
        hand_over(p).start()
        return c

    def handed(p, c):
        hand_over(p).wait_recv()
        return c

    def handed_off(p, c):
        hand_over(p).wait_send()
        return c

    lax.fori_loop(1, n_z, pass_on, 0)
    lax.fori_loop(0, n_z, handed, 0)
    gain_received()
    raw = jnp.concatenate([feats[i] for i in range(n_vocab)], axis=1).astype(jnp.float32)
    scale = jnp.concatenate([gains[i, 0:1] for i in range(n_vocab)], axis=1)
    mean_square = jnp.sum(raw * raw, axis=1, keepdims=True) / width
    own = (raw * lax.rsqrt(mean_square + EPSILON) * scale).astype(jnp.bfloat16)
    for k in range(2):
        part = own[:, k * half_width : (k + 1) * half_width]
        rows_x[0, k, 0, 0] = part[:HALF]
        rows_x[0, k, 1, 0] = part[HALF:]

    def across(order, p):
        if order == 0:
            return ((x + p) % side) * side + y
        return x * side + (y + p) % side

    def first(order, j):
        return pltpu.make_async_remote_copy(
            src_ref=rows_x.at[0, core, order, 0], dst_ref=rows_x.at[j, core, order, 0],
            send_sem=one_s.at[order, j], recv_sem=one_r.at[order, j],
            device_id={"seq": across(order, j)}, device_id_type=MESH,
        )

    def second(order, j, p):
        return pltpu.make_async_remote_copy(
            src_ref=rows_x.at[j, core, order, 0], dst_ref=rows_x.at[j, core, order, p],
            send_sem=two_s.at[order, j, p], recv_sem=two_r.at[order, j, p],
            device_id={"seq": across(1 - order, p)}, device_id_type=MESH,
        )

    def over(kind, order, j, p):
        at = rows_x.at[j, kind, order, p]
        return pltpu.make_async_remote_copy(
            src_ref=at, dst_ref=at, send_sem=fwd_s.at[order, j, p], recv_sem=fwd_r.at[order, j, p],
            device_id={"vocab": sibling}, device_id_type=MESH,
        )

    near = [p for d in range(1, side // 2 + 1) for p in sorted({d, side - d})]
    for j in near:
        for order in range(2):
            first(order, j).start()
    for p in near:
        for order in range(2):
            second(order, 0, p).start()
    for j in near:
        for order in range(2):
            first(order, j).wait_recv()
            for p in near:
                second(order, j, p).start()
            over(core, order, j, 0).start()

    loads[3].wait()
    level[pl.ds(total, slots)] = jnp.zeros((slots, entries), jnp.int32)
    columns = 256 if entries % 256 == 0 else entries

    def row_of(order, j, p):
        if order == 0:
            return ((x + side - j) % side * side + (y + side - p) % side) * rows
        return ((x + side - p) % side * side + (y + side - j) % side) * rows + HALF

    def product(j, k, i):
        at = pl.ds(pl.multiple_of(i * columns, columns), columns)
        return at, lax.dot_general(
            rows_x[j, k].reshape(block_rows, half_width),
            head[at, pl.ds(pl.multiple_of(k * half_width, half_width), half_width)],
            (((1,), (1,)), ((), ())),
            preferred_element_type=jnp.float32,
        )

    def begin_block(j):
        def some(i, c):
            at, logits = product(j, core, i)
            partial[:, at] = logits
            return c

        lax.fori_loop(0, entries // columns, some, 0)

    def end_block(j):
        def some(i, total_exp):
            at, logits = product(j, 1 - core, i)
            bent = jnp.tanh((logits + partial[:, at]) / SOFT_CAP)
            code = jnp.round(bent * CODE).astype(jnp.int32)
            for order in range(2):
                for p in range(side):
                    low = (order * side + p) * HALF
                    level[pl.ds(pl.multiple_of(row_of(order, j, p), HALF), HALF), at] = code[low : low + HALF]
            e = jnp.exp(SOFT_CAP * bent)
            for c in range(0, columns, 128):
                total_exp += e[:, c : c + 128]
            return total_exp

        total_exp = lax.fori_loop(0, entries // columns, some, jnp.zeros((block_rows, 128), jnp.float32))
        summed = jnp.broadcast_to(jnp.sum(total_exp, axis=1, keepdims=True), total_exp.shape)
        for order in range(2):
            for p in range(side):
                low = (order * side + p) * HALF
                expo[pl.ds(pl.multiple_of(row_of(order, j, p), HALF), HALF)] = summed[low : low + HALF]

    for j in [0] + near:
        for p in near:
            for order in range(2):
                second(order, j, p).wait_recv()
                over(core, order, j, p).start()
        begin_block(j)
        for p in near + ([0] if j else []):
            for order in range(2):
                over(1 - core, order, j, p).wait_recv()
        end_block(j)

    square_eye = iota((128, 128), 0) == iota((128, 128), 1)
    lines = [
        jnp.sum(jnp.where(square_eye, expo[i * 128 : (i + 1) * 128], 0.0), axis=0, keepdims=True)
        for i in range(total // 128)
    ]
    lines.append(jnp.zeros((8 - len(lines), 128), jnp.float32))
    sums_a[pl.ds(s, 1)] = jnp.concatenate(lines, axis=0)[None]
    sma_start, sma_received, sma_sent = exchange(
        n_seq, "seq", seq_peer, lambda p: sums_a.at[s], sums_a.at[s], sums_a.at[pl.ds(0, n_seq - 1)], sma_sem
    )
    sma_start()


    def fill(p):
        start = jnp.sum(jnp.where(group < seq_peer(p), cnt[...], 0), axis=0)[0:1, 0:1]
        for c in range(0, entries, 128):
            window = level[:, c : c + 128]
            bit = 1 << (total.bit_length() - 2)
            while bit:
                left = bit - 1 + slots if bit > 8 else slots + 8
                left = (left + 7) // 8 * 8
                if bit >= 8:
                    window = jnp.where(start & bit != 0, window[bit : bit + left], window[:left])
                else:
                    window = jnp.where(start & bit != 0, pltpu.roll(window, left - bit, axis=0), window)
                bit //= 2
            send[pl.ds(p, 1), :, c : c + 128] = window[:slots].astype(jnp.int16)[None]

    out_start, out_received, out_sent = exchange(
        n_seq, "seq", seq_peer, lambda p: send.at[p], codes_ref.at[s], codes_ref.at[pl.ds(0, n_seq - 1)], out_sem, fill
    )

    out_start()
    fill(0)
    keep = pltpu.make_async_copy(send.at[0], codes_ref.at[s], own_sem)
    keep.start()

    sma_received()
    sums_b[pl.ds(v, 1)] = jnp.sum(sums_a[...], axis=0)[None]
    smb_start, smb_received, smb_sent = exchange(
        n_vocab, "vocab", vocab_peer, lambda p: sums_b.at[v], sums_b.at[v], sums_b.at[pl.ds(0, n_vocab - 1)], smb_sem
    )
    smb_start()
    smb_received()
    partition = jnp.sum(sums_b[...], axis=0)
    mine = jnp.zeros((slots, 1), jnp.float32)
    for i in range(total // 128):
        hit = iota((slots, 128), 1) + 128 * i == offset + iota((slots, 128), 0)
        mine += jnp.sum(jnp.where(hit, partition[i : i + 1], 0.0), axis=1, keepdims=True)
    logs_ref[...] = jnp.broadcast_to(jnp.log(jnp.where(mine > 0.0, mine, 1.0)), logs_ref.shape)

    cnt_sent()
    gain_sent()
    plc_sent()
    lax.fori_loop(1, n_z, set_off, 0)
    lax.fori_loop(0, n_z, handed_off, 0)
    for order in range(2):
        for j in near:
            first(order, j).wait_send()
            over(core, order, j, 0).wait_send()
        for j in [0] + near:
            for p in near:
                second(order, j, p).wait_send()
                over(core, order, j, p).wait_send()
    sma_sent()
    smb_sent()
    keep.wait()
    out_received()
    out_sent()


def decode(counts_ref, codes_ref, logs_ref, out_ref):
    blocks, slots, entries = codes_ref.shape
    live = iota((slots, entries), 0) < counts_ref[0]
    for i in range(blocks):
        capped = codes_ref[i].astype(jnp.float32) * (SOFT_CAP / CODE)
        out_ref[:, i * entries : (i + 1) * entries] = jnp.where(live, capped - logs_ref[:, :1], 0.0)


def solution(mesh):
    n_seq, n_vocab = mesh.shape["seq"], mesh.shape["vocab"]
    side = int(round(n_seq**0.5))

    def local(hidden, picks, counts, norm_gain, head_weight):
        slots = picks.shape[1]
        entries, width = head_weight.shape
        positions, features = hidden.shape[1:]
        total = n_seq * slots // 2
        rows = total // n_seq
        dma = lambda *shape: [pltpu.SemaphoreType.DMA(shape)] * 2
        vmem = pl.BlockSpec(memory_space=pltpu.VMEM)
        hbm = pl.BlockSpec(memory_space=pl.ANY)
        codes, logs = pl.pallas_call(
            functools.partial(kernel, (n_seq, n_vocab, side, slots, total)),
            out_shape=(
                jax.ShapeDtypeStruct((n_seq, slots, entries), jnp.int16),
                jax.ShapeDtypeStruct((slots, 128), jnp.float32),
            ),
            in_specs=[hbm, hbm, pl.BlockSpec(memory_space=pltpu.SMEM), hbm, hbm],
            out_specs=(hbm, vmem),
            scratch_shapes=[
                pltpu.VMEM((features, positions), jnp.bfloat16),
                pltpu.VMEM((1, slots), jnp.int32),
                pltpu.VMEM((features,), jnp.float32),
                pltpu.VMEM((entries, width), jnp.bfloat16),
                pltpu.VMEM((n_seq, 8, 128), jnp.int32),
                pltpu.VMEM((n_vocab, 8, features), jnp.float32),
                pltpu.VMEM((n_seq, rows, features), jnp.bfloat16),
                pltpu.VMEM((n_seq, rows, features), jnp.bfloat16),
                pltpu.VMEM((n_vocab, rows, features), jnp.bfloat16),
                pltpu.VMEM((side, 2, 2, side, HALF, width // 2), jnp.bfloat16),
                pltpu.VMEM((2 * side * HALF, entries), jnp.float32),
                pltpu.VMEM((total + slots, entries), jnp.int32),
                pltpu.VMEM((total, 128), jnp.float32),
                pltpu.VMEM((n_seq, slots, entries), jnp.int16),
                pltpu.VMEM((n_seq, 8, 128), jnp.float32),
                pltpu.VMEM((n_vocab, 8, 128), jnp.float32),
                pltpu.SemaphoreType.DMA((4,)),
                pltpu.SemaphoreType.DMA,
                *[pltpu.SemaphoreType.DMA((2,))] * 6,
                *dma(n_vocab // 2),
                *dma(n_vocab // 2),
                *dma(2, side),
                *dma(2, side, side),
                *dma(2, side, side),
            ],
            compiler_params=pltpu.CompilerParams(
                collective_id=0, has_side_effects=True, vmem_limit_bytes=48 << 20
            ),
            cost_estimate=pl.CostEstimate(
                flops=2 * total * entries * width, bytes_accessed=2 * entries * width, transcendentals=2 * total * entries
            ),
        )(jnp.swapaxes(hidden[0], 0, 1), picks, counts, norm_gain, head_weight)
        step = max(1, n_seq // 4)
        return pl.pallas_call(
            decode,
            grid=(n_seq // step,),
            out_shape=jax.ShapeDtypeStruct((slots, n_seq * entries), jnp.float32),
            in_specs=[
                pl.BlockSpec(memory_space=pltpu.SMEM),
                pl.BlockSpec((step, slots, entries), lambda i: (i, 0, 0)),
                pl.BlockSpec((slots, 128), lambda i: (0, 0)),
            ],
            out_specs=pl.BlockSpec((slots, step * entries), lambda i: (0, i)),
        )(counts, codes, logs)

    in_specs = (
        P("seq", None, "vocab"),
        P("seq", None),
        P("seq"),
        P("vocab"),
        P(("vocab", "seq"), None),
    )
    return jax.shard_map(local, mesh=mesh, in_specs=in_specs, out_specs=P("seq", "vocab"), check_vma=False)
```

time: 100 us -> 91.6 us (0.916)
  the two profiles are of different devices: /device:TPU:60 before, /device:TPU:61 now
where the time goes in v2:
time: 91.6 us; the launch traced here: 91.4 us
  Pallas kernels  86.4 us (94%)
  local copies, waits for them, and re-layouts  4.35 us (5%)
    pallas_call x1, Pallas kernels, local(): pl.pallas_call(functools.partial(kernel, (n_seq, n_vocab, side, slots, to...  82.3 us
    unnamed x10, local copies, waits for them, and re-layouts  4.35 us
    pallas_call x1, Pallas kernels, local(): pl.pallas_call(decode, grid=(n_seq // step,), out_shape=jax.ShapeDtypeStr...  4.1 us

profile of v2, /device:TPU:61, one launch (start us, length us, event | category | flops | bytes accessed | tf_op | source)
XLA Modules:
  0.0 91.4 jit_solution(3469881008071970701)
XLA Ops:
  0.7 0.0 copy-start.2
  0.7 1.3 %copy-done.2 = bf16[1,2048,288]{1,2,0:T(8,128)(2,1)S(1)} copy-done((bf16[1,2048,288]{1,2,0:T(8,128)(2,1)S(1)}, bf16[1,2048,288]{1,2,0:T(8,128)(2,1)}, u32[]{:S(2)}) %copy-start.2) | copy-done | bytes 1179672
  1.9 0.0 copy-start.3
  1.9 0.7 copy-done.3
  2.6 0.0 copy-start.4
  2.6 0.7 copy-done.4
  3.3 82.3 %shard_map.55 = (s16[16,64,768]{2,1,0:T(8,128)(2,1)S(1)}, f32[64,128]{1,0:T(8,128)S(1)}) custom-call(bf16[288,2048]{1,0:T(8,128)(2,1)S(1)} %bitcast.3, s32[1,64]{1,0:T(1,128)S(1)} %copy-done.4, s32[1]{0:T(128)S(6)} %copy.6.counts_ref, f32[288]{0:T(512)S(1)} %copy-done.3, bf16[768,4608]{1,0:T(8,128)(2,1)} %head_ref.1), custom_call_target="tpu_custom_call" | custom-call | flops 3623878656 | bytes 7077888 | tf_op jit(solution)/shard_map/pallas_call | solution.py:411
  85.5 0.0 copy-start
  85.6 1.1 %copy-done = s16[16,64,768]{2,1,0:T(8,128)(2,1)} copy-done((s16[16,64,768]{2,1,0:T(8,128)(2,1)}, s16[16,64,768]{2,1,0:T(8,128)(2,1)S(1)}, u32[]{:S(2)}) %copy-start) | copy-done | bytes 1572888
  86.7 0.0 copy-start.1
  86.7 0.6 copy-done.1
  87.3 4.1 %shard_map.56 = f32[64,12288]{1,0:T(8,128)} custom-call(s32[1]{0:T(128)S(6)} %copy.6.counts_ref, s16[16,64,768]{2,1,0:T(8,128)(2,1)} %copy-done, f32[64,128]{1,0:T(8,128)} %copy-done.1), custom_call_target="tpu_custom_call" | custom-call | tf_op jit(solution)/shard_map/pallas_call | solution.py:453
Async XLA Ops:
  0.7 1.3 %copy-start.2 = (bf16[1,2048,288]{1,2,0:T(8,128)(2,1)S(1)}, bf16[1,2048,288]{1,2,0:T(8,128)(2,1)}, u32[]{:S(2)}) copy-start(bf16[1,2048,288]{1,2,0:T(8,128)(2,1)} %param.5) | copy-start | bytes 3538948
  1.9 0.7 copy-start.3
  2.6 0.7 copy-start.4
  85.5 1.2 %copy-start = (s16[16,64,768]{2,1,0:T(8,128)(2,1)}, s16[16,64,768]{2,1,0:T(8,128)(2,1)S(1)}, u32[]{:S(2)}) copy-start(s16[16,64,768]{2,1,0:T(8,128)(2,1)S(1)} %get-tuple-element.7.codes_ref) | copy-start | bytes 4718596
  86.7 0.6 copy-start.1

commit v3 on v2

v3 whole, which is shorter than its diff:
```python
import functools

import jax
import jax.numpy as jnp
from jax import lax
from jax.experimental import pallas as pl
from jax.experimental.pallas import tpu as pltpu
from jax.sharding import PartitionSpec as P

SOFT_CAP = 30.0
EPSILON = 1e-06
CODE = 32767.0
HALF = 16
COLUMNS = 256
VMEM_BYTES = 63 << 20
MESH = pl.DeviceIdType.MESH


def iota(shape, dim):
    return lax.broadcasted_iota(jnp.int32, shape, dim)


def kernel(
    dims,
    hidden_ref,
    picks_ref,
    counts_ref,
    gain_ref,
    head_ref,
    codes_ref,
    terms_ref,
    hidden,
    picks,
    gain,
    head,
    cnt,
    gains,
    squares,
    place,
    placed,
    block_out,
    feats,
    rows_x,
    partial,
    level,
    expo,
    send,
    terms,
    sums_a,
    sums_b,
    in_sem,
    terms_sem,
    own_sem,
    cnt_sem,
    gain_sem,
    sqs_sem,
    plc_sem,
    fea_sem,
    sma_sem,
    smb_sem,
    out_s, out_r,
    one_s, one_r,
    two_s, two_r,
    fwd_s, fwd_r,
):
    n_seq, n_vocab, side, slots, total = dims
    rows = total // n_seq
    width = head_ref.shape[1]
    entries = head_ref.shape[0]
    features = hidden_ref.shape[0]
    block_rows = 2 * side * HALF
    half_width = width // 2
    n_z = n_vocab // 2
    s = lax.axis_index("seq")
    v = lax.axis_index("vocab")
    x, y = s // side, s % side
    z, core = v // 2, v % 2
    sibling = 2 * z + (1 - core)

    def seq_peer(p):
        return (s + p) % n_seq

    def vocab_peer(p):
        return (v + p) % n_vocab

    loads = [
        pltpu.make_async_copy(ref, to, in_sem.at[i])
        for i, (ref, to) in enumerate(
            [(hidden_ref, hidden), (picks_ref, picks), (gain_ref, gain), (head_ref, head)]
        )
    ]
    for load in loads:
        load.start()

    barrier = pltpu.get_barrier_semaphore()

    def greet_seq(p, c):
        pl.semaphore_signal(barrier, inc=1, device_id={"seq": seq_peer(p)}, device_id_type=MESH)
        return c

    def greet_vocab(p, c):
        pl.semaphore_signal(barrier, inc=1, device_id={"vocab": vocab_peer(p)}, device_id_type=MESH)
        return c

    lax.fori_loop(1, n_seq, greet_seq, 0)
    lax.fori_loop(1, n_vocab, greet_vocab, 0)
    pl.semaphore_wait(barrier, n_seq + n_vocab - 2)

    def hops(p, size):
        return min(p, size - p)

    seq_steps = sorted(
        ((a, b) for a in range(side) for b in range(side) if a or b),
        key=lambda step: hops(step[0], side) + hops(step[1], side),
    )

    def exchange(axis, peers, src, dst, many, sems):
        def copy(peer, src, dst):
            return pltpu.make_async_remote_copy(
                src_ref=src, dst_ref=dst, send_sem=sems.at[0], recv_sem=sems.at[1],
                device_id={axis: peer}, device_id_type=MESH,
            )

        def start():
            for peer in peers:
                copy(peer, src(peer), dst).start()

        def received():
            copy(peers[0], many, many).wait_recv()

        def sent():
            copy(peers[0], many, many).wait_send()

        return start, received, sent

    seq_peers = [(x + a) % side * side + (y + b) % side for a, b in seq_steps]
    vocab_peers = [vocab_peer(p) for p in sorted(range(1, n_vocab), key=lambda p: -hops(p, n_vocab))]

    cnt[pl.ds(s, 1)] = jnp.full((1, 8, 128), counts_ref[0], jnp.int32)
    cnt_start, cnt_received, cnt_sent = exchange(
        "seq", seq_peers, lambda peer: cnt.at[s], cnt.at[s], cnt.at[pl.ds(0, n_seq - 1)], cnt_sem
    )
    cnt_start()

    loads[0].wait()
    loads[1].wait()
    one_hot = (iota((hidden.shape[1], slots), 0) == picks[...]).astype(jnp.bfloat16)
    selected = jnp.dot(hidden[...], one_hot, preferred_element_type=jnp.float32).astype(jnp.bfloat16)

    loads[2].wait()
    line = gain[...].reshape(1, features)
    line = jnp.concatenate([line, jnp.zeros((1, -features % 128), jnp.float32)], axis=1)
    lines = [line[:, c : c + 128] for c in range(0, line.shape[1], 128)]
    lines.append(jnp.zeros((8 - len(lines), 128), jnp.float32))
    gains[pl.ds(v, 1)] = jnp.concatenate(lines, axis=0)[None]
    gain_start, gain_received, gain_sent = exchange(
        "vocab", vocab_peers, lambda peer: gains.at[v], gains.at[v], gains.at[pl.ds(0, n_vocab - 1)], gain_sem
    )
    gain_start()

    cnt_received()
    group = iota((n_seq, 8, 128), 0)
    every = cnt[...]
    offset = jnp.sum(jnp.where(group < s, every, 0), axis=0)[0:1, 0:1]
    count = jnp.sum(jnp.where(group == s, every, 0), axis=0)[0:1, 0:1]

    slot = iota((total, slots), 1)
    placing = ((iota((total, slots), 0) == offset + slot) & (slot < count)).astype(jnp.bfloat16)

    compact = lax.dot_general(
        placing, selected, (((1,), (1,)), ((), ())), preferred_element_type=jnp.float32
    ).astype(jnp.bfloat16)
    place[...] = compact.reshape(n_seq, rows, features)
    plc_start, plc_received, plc_sent = exchange(
        "seq", seq_peers, lambda peer: place.at[peer], placed.at[s], placed.at[pl.ds(0, n_seq - 1)], plc_sem
    )
    plc_start()
    placed[pl.ds(s, 1)] = place[pl.ds(s, 1)]
    plc_received()
    block = jnp.sum(placed[...].astype(jnp.float32), axis=0).astype(jnp.bfloat16)

    wide = block.astype(jnp.float32)
    row_eye = iota((rows, 128), 0) == iota((rows, 128), 1)
    square = jnp.sum(jnp.where(row_eye, jnp.sum(wide * wide, axis=1, keepdims=True), 0.0), axis=0, keepdims=True)
    squares[pl.ds(v, 1)] = jnp.broadcast_to(square, (8, 128))[None]
    sqs_start, sqs_received, sqs_sent = exchange(
        "vocab", vocab_peers, lambda peer: squares.at[v], squares.at[v], squares.at[pl.ds(0, n_vocab - 1)], sqs_sem
    )

    part_of = z // (n_z // 2)
    kept = core == part_of
    mine = v - part_of * n_z

    def along(p, src, dst):
        return pltpu.make_async_remote_copy(
            src_ref=src, dst_ref=dst, send_sem=fea_sem.at[0], recv_sem=fea_sem.at[1],
            device_id={"vocab": 2 * ((z + p) % n_z) + part_of}, device_id_type=MESH,
        )

    block_out[...] = block
    for p in sorted(range(1, n_z), key=lambda p: -hops(p, n_z)):
        along(p, block_out, feats.at[mine]).start()

    @pl.when(kept)
    def _():
        feats[pl.ds(mine, 1)] = block[None]

    @pl.when(jnp.logical_not(kept))
    def _():
        along(0, block_out, feats.at[mine]).start()

    sqs_start()

    @pl.when(kept)
    def _():
        many = feats.at[pl.ds(0, n_z - 1)]
        along(1, many, many).wait_recv()

    @pl.when(jnp.logical_not(kept))
    def _():
        along(1, feats, feats).wait_recv()

    gain_received()
    sqs_received()
    raw = jnp.concatenate([feats[i] for i in range(n_z)], axis=1).astype(jnp.float32)
    held = gains[pl.ds(core * n_z, n_z)]
    scale = jnp.concatenate(
        [held[i, c // 128 : c // 128 + 1, : min(128, features - c)] for i in range(n_z) for c in range(0, features, 128)],
        axis=1,
    )
    mean_square = jnp.sum(squares[...], axis=0)[0:1] / width
    mean_square = jnp.sum(jnp.where(row_eye, mean_square, 0.0), axis=1, keepdims=True)
    own = (raw * lax.rsqrt(mean_square + EPSILON) * scale).astype(jnp.bfloat16)
    rows_x[0, pl.ds(core, 1), 0, 0] = own[:HALF][None]
    rows_x[0, pl.ds(core, 1), 1, 0] = own[HALF:][None]

    def across(order, p):
        if order == 0:
            return ((x + p) % side) * side + y
        return x * side + (y + p) % side

    def first(order, j):
        return pltpu.make_async_remote_copy(
            src_ref=rows_x.at[0, core, order, 0], dst_ref=rows_x.at[j, core, order, 0],
            send_sem=one_s.at[order, j], recv_sem=one_r.at[order, j],
            device_id={"seq": across(order, j)}, device_id_type=MESH,
        )

    def second(order, j, p):
        return pltpu.make_async_remote_copy(
            src_ref=rows_x.at[j, core, order, 0], dst_ref=rows_x.at[j, core, order, p],
            send_sem=two_s.at[order, j, p], recv_sem=two_r.at[order, j, p],
            device_id={"seq": across(1 - order, p)}, device_id_type=MESH,
        )

    def over(kind, order, j, p):
        at = rows_x.at[j, kind, order, p]
        return pltpu.make_async_remote_copy(
            src_ref=at, dst_ref=at, send_sem=fwd_s.at[order, j, p], recv_sem=fwd_r.at[order, j, p],
            device_id={"vocab": sibling}, device_id_type=MESH,
        )

    near = [p for d in range(1, side // 2 + 1) for p in sorted({d, side - d})]
    for j in near:
        for order in range(2):
            first(order, j).start()
    for p in near:
        for order in range(2):
            second(order, 0, p).start()
    for order in range(2):
        over(core, order, 0, 0).start()
    for j in near:
        for order in range(2):
            first(order, j).wait_recv()
            for p in near:
                second(order, j, p).start()
            over(core, order, j, 0).start()

    loads[3].wait()
    level[pl.ds(total, slots)] = jnp.zeros((slots, entries), jnp.int32)
    rounds = entries // COLUMNS

    def row_of(order, j, p):
        if order == 0:
            return ((x + side - j) % side * side + (y + side - p) % side) * rows
        return ((x + side - p) % side * side + (y + side - j) % side) * rows + HALF

    def product(j, k, i):
        at = pl.ds(pl.multiple_of(i * COLUMNS, COLUMNS), COLUMNS)
        return at, lax.dot_general(
            rows_x[j, k].reshape(block_rows, half_width),
            head[at, pl.ds(pl.multiple_of(k * half_width, half_width), half_width)],
            (((1,), (1,)), ((), ())),
            preferred_element_type=jnp.float32,
        )

    def fill(i):
        at = i * COLUMNS

        def one(g, c):
            start = jnp.sum(jnp.where(group < g, cnt[...], 0), axis=0)[0:1, 0:1]
            for low in range(0, COLUMNS, 128):
                window = level[:, pl.ds(pl.multiple_of(at + low, 128), 128)]
                bit = 1 << (total.bit_length() - 2)
                while bit:
                    left = bit - 1 + slots if bit > 8 else slots + 8
                    left = (left + 7) // 8 * 8
                    if bit >= 8:
                        window = jnp.where(start & bit != 0, window[bit : bit + left], window[:left])
                    else:
                        window = jnp.where(start & bit != 0, pltpu.roll(window, left - bit, axis=0), window)
                    bit //= 2
                send[pl.ds(i, 1), pl.ds(g, 1), :, low : low + 128] = window[:slots].astype(jnp.int16)[None, None]
            return c

        lax.fori_loop(0, n_seq, one, 0)
        keep(i).start()

    def keep(i):
        return pltpu.make_async_copy(send.at[i, s], codes_ref.at[i, s], own_sem.at[i])

    def returned(i, peer, src, dst):
        return pltpu.make_async_remote_copy(
            src_ref=src, dst_ref=dst, send_sem=out_s.at[i], recv_sem=out_r.at[i],
            device_id={"seq": peer}, device_id_type=MESH,
        )

    def give(i):
        for peer in seq_peers:
            returned(i, peer, send.at[i, peer], codes_ref.at[i, s]).start()

    def all_returned(i):
        many = codes_ref.at[i, pl.ds(0, n_seq - 1)]
        return returned(i, seq_peers[0], many, many)

    last = near[-1]

    def begin_block(j):
        def some(i, c):
            at, logits = product(j, core, i)
            partial[:, at] = logits
            return c

        lax.fori_loop(0, rounds, some, 0)

    def end_block(j):
        def some(i, total_exp):
            at, logits = product(j, 1 - core, i)
            bent = jnp.tanh((logits + partial[:, at]) / SOFT_CAP)
            code = jnp.round(bent * CODE).astype(jnp.int32)
            for order in range(2):
                for p in range(side):
                    low = (order * side + p) * HALF
                    level[pl.ds(pl.multiple_of(row_of(order, j, p), HALF), HALF), at] = code[low : low + HALF]
            e = jnp.exp(SOFT_CAP * bent)
            for c in range(0, COLUMNS, 128):
                total_exp += e[:, c : c + 128]
            if j == last:
                fill(i)

                @pl.when(i == 0)
                def _():
                    give(0)

            return total_exp

        total_exp = lax.fori_loop(0, rounds, some, jnp.zeros((block_rows, 128), jnp.float32))
        summed = jnp.broadcast_to(jnp.sum(total_exp, axis=1, keepdims=True), total_exp.shape)
        for order in range(2):
            for p in range(side):
                low = (order * side + p) * HALF
                expo[pl.ds(pl.multiple_of(row_of(order, j, p), HALF), HALF)] = summed[low : low + HALF]

    for j in [0] + near:
        for p in near:
            for order in range(2):
                second(order, j, p).wait_recv()
                over(core, order, j, p).start()
        begin_block(j)
        for p in [0] + near:
            for order in range(2):
                over(1 - core, order, j, p).wait_recv()
        end_block(j)

    square_eye = iota((128, 128), 0) == iota((128, 128), 1)
    lines = [
        jnp.sum(jnp.where(square_eye, expo[i * 128 : (i + 1) * 128], 0.0), axis=0, keepdims=True)
        for i in range(total // 128)
    ]
    lines.append(jnp.zeros((8 - len(lines), 128), jnp.float32))
    sums_a[pl.ds(s, 1)] = jnp.concatenate(lines, axis=0)[None]
    sma_start, sma_received, sma_sent = exchange(
        "seq", seq_peers, lambda peer: sums_a.at[s], sums_a.at[s], sums_a.at[pl.ds(0, n_seq - 1)], sma_sem
    )
    sma_start()

    for i in range(1, rounds):
        give(i)

    sma_received()
    sums_b[pl.ds(v, 1)] = jnp.sum(sums_a[...], axis=0)[None]
    smb_start, smb_received, smb_sent = exchange(
        "vocab", vocab_peers, lambda peer: sums_b.at[v], sums_b.at[v], sums_b.at[pl.ds(0, n_vocab - 1)], smb_sem
    )
    smb_start()
    smb_received()
    partition = jnp.sum(sums_b[...], axis=0)
    total_of = jnp.zeros((slots, 1), jnp.float32)
    for i in range(total // 128):
        hit = iota((slots, 128), 1) + 128 * i == offset + iota((slots, 128), 0)
        total_of += jnp.sum(jnp.where(hit, partition[i : i + 1], 0.0), axis=1, keepdims=True)
    live = iota((slots, 128), 0) < count
    terms[0] = jnp.where(live, SOFT_CAP / CODE, 0.0)
    terms[1] = jnp.where(live, jnp.log(jnp.where(total_of > 0.0, total_of, 1.0)), 0.0)
    write_terms = pltpu.make_async_copy(terms, terms_ref, terms_sem)
    write_terms.start()

    cnt_sent()
    gain_sent()
    plc_sent()
    sqs_sent()

    @pl.when(kept)
    def _():
        many = feats.at[pl.ds(0, n_z - 1)]
        along(1, many, many).wait_send()

    @pl.when(jnp.logical_not(kept))
    def _():
        along(1, feats, feats).wait_send()

    for order in range(2):
        over(core, order, 0, 0).wait_send()
        for j in near:
            first(order, j).wait_send()
            over(core, order, j, 0).wait_send()
        for j in [0] + near:
            for p in near:
                second(order, j, p).wait_send()
                over(core, order, j, p).wait_send()
    sma_sent()
    smb_sent()
    write_terms.wait()
    for i in range(rounds):
        keep(i).wait()
        all_returned(i).wait()


def decode(codes_ref, terms_ref, out_ref, codes, terms, result, codes_sem, terms_sem, out_sem):
    rounds, n_seq, slots, _ = codes_ref.shape
    entries = rounds * COLUMNS
    steps = 4
    step = n_seq // steps
    take_terms = pltpu.make_async_copy(terms_ref, terms, terms_sem)
    take_terms.start()

    def take(k):
        at = pl.ds(k * step, step)
        return pltpu.make_async_copy(codes_ref.at[:, at], codes.at[:, at], codes_sem.at[k])

    def put(k):
        at = pl.ds(k * step * entries, step * entries)
        return pltpu.make_async_copy(result.at[:, at], out_ref.at[:, at], out_sem.at[k])

    for k in range(steps):
        take(k).start()
    take_terms.wait()
    for k in range(steps):
        take(k).wait()
        for g in range(k * step, (k + 1) * step):
            for i in range(rounds):
                for low in range(0, COLUMNS, 128):
                    at = g * entries + i * COLUMNS + low
                    code = codes[i, g, :, low : low + 128].astype(jnp.int32).astype(jnp.float32)
                    result[:, at : at + 128] = code * terms[0] - terms[1]
        put(k).start()
    for k in range(steps):
        put(k).wait()


def solution(mesh):
    n_seq, n_vocab = mesh.shape["seq"], mesh.shape["vocab"]
    side = int(round(n_seq**0.5))

    def local(hidden, picks, counts, norm_gain, head_weight):
        slots = picks.shape[1]
        entries, width = head_weight.shape
        positions, features = hidden.shape[1:]
        total = n_seq * slots // 2
        rows = total // n_seq
        dma = lambda *shape: [pltpu.SemaphoreType.DMA(shape)] * 2
        hbm = pl.BlockSpec(memory_space=pltpu.HBM)
        codes, terms = pl.pallas_call(
            functools.partial(kernel, (n_seq, n_vocab, side, slots, total)),
            out_shape=(
                jax.ShapeDtypeStruct((entries // COLUMNS, n_seq, slots, COLUMNS), jnp.int16),
                jax.ShapeDtypeStruct((2, slots, 128), jnp.float32),
            ),
            in_specs=[hbm, hbm, pl.BlockSpec(memory_space=pltpu.SMEM), hbm, hbm],
            out_specs=(hbm, hbm),
            scratch_shapes=[
                pltpu.VMEM((features, positions), jnp.bfloat16),
                pltpu.VMEM((1, slots), jnp.int32),
                pltpu.VMEM((features,), jnp.float32),
                pltpu.VMEM((entries, width), jnp.bfloat16),
                pltpu.VMEM((n_seq, 8, 128), jnp.int32),
                pltpu.VMEM((n_vocab, 8, 128), jnp.float32),
                pltpu.VMEM((n_vocab, 8, 128), jnp.float32),
                pltpu.VMEM((n_seq, rows, features), jnp.bfloat16),
                pltpu.VMEM((n_seq, rows, features), jnp.bfloat16),
                pltpu.VMEM((rows, features), jnp.bfloat16),
                pltpu.VMEM((n_vocab // 2, rows, features), jnp.bfloat16),
                pltpu.VMEM((side, 2, 2, side, HALF, width // 2), jnp.bfloat16),
                pltpu.VMEM((2 * side * HALF, entries), jnp.float32),
                pltpu.VMEM((total + slots, entries), jnp.int32),
                pltpu.VMEM((total, 128), jnp.float32),
                pltpu.VMEM((entries // COLUMNS, n_seq, slots, COLUMNS), jnp.int16),
                pltpu.VMEM((2, slots, 128), jnp.float32),
                pltpu.VMEM((n_seq, 8, 128), jnp.float32),
                pltpu.VMEM((n_vocab, 8, 128), jnp.float32),
                pltpu.SemaphoreType.DMA((4,)),
                pltpu.SemaphoreType.DMA,
                pltpu.SemaphoreType.DMA((entries // COLUMNS,)),
                *[pltpu.SemaphoreType.DMA((2,))] * 7,
                *dma(entries // COLUMNS),
                *dma(2, side),
                *dma(2, side, side),
                *dma(2, side, side),
            ],
            compiler_params=pltpu.CompilerParams(
                collective_id=0, has_side_effects=True, vmem_limit_bytes=VMEM_BYTES
            ),
            cost_estimate=pl.CostEstimate(
                flops=2 * total * entries * width, bytes_accessed=2 * entries * width, transcendentals=2 * total * entries
            ),
        )(jnp.swapaxes(hidden[0], 0, 1), picks, counts, norm_gain, head_weight)
        return pl.pallas_call(
            decode,
            out_shape=jax.ShapeDtypeStruct((slots, n_seq * entries), jnp.float32),
            in_specs=[hbm, hbm],
            out_specs=hbm,
            scratch_shapes=[
                pltpu.VMEM(codes.shape, codes.dtype),
                pltpu.VMEM(terms.shape, terms.dtype),
                pltpu.VMEM((slots, n_seq * entries), jnp.float32),
                pltpu.SemaphoreType.DMA((4,)),
                pltpu.SemaphoreType.DMA,
                pltpu.SemaphoreType.DMA((4,)),
            ],
            compiler_params=pltpu.CompilerParams(vmem_limit_bytes=VMEM_BYTES),
        )(codes, terms)
    in_specs = (
        P("seq", None, "vocab"),
        P("seq", None),
        P("seq"),
        P("vocab"),
        P(("vocab", "seq"), None),
    )
    return jax.shard_map(local, mesh=mesh, in_specs=in_specs, out_specs=P("seq", "vocab"), check_vma=False)
```

time: 91.6 us -> 81 us (0.88)
  the two profiles are of different devices: /device:TPU:61 before, /device:TPU:1 now
where the time goes in v3:
time: 81 us; the launch traced here: 80.9 us
  Pallas kernels  80.3 us (99%)
    pallas_call x1, Pallas kernels, local(): pl.pallas_call(functools.partial(kernel, (n_seq, n_vocab, side, slots, to...  77.2 us
    pallas_call x1, Pallas kernels, local(): pl.pallas_call(decode, out_shape=jax.ShapeDtypeStruct((slots, n_seq * ent...  3.03 us

profile of v3, /device:TPU:1, one launch (start us, length us, event | category | flops | bytes accessed | tf_op | source)
XLA Modules:
  0.0 80.9 jit_solution(11004582517175440010)
XLA Ops:
  0.7 77.2 %shard_map.55 = (s16[3,16,64,256]{3,2,1,0:T(8,128)(2,1)}, f32[2,64,128]{2,1,0:T(8,128)}) custom-call(bf16[288,2048]{1,0:T(8,128)(2,1)} %bitcast.3, s32[1,64]{1,0:T(1,128)} %picks_ref.1, s32[1]{0:T(128)S(6)} %copy.6.counts_ref, f32[288]{0:T(512)} %gain_ref.1, bf16[768,4608]{1,0:T(8,128)(2,1)} %head_ref.1), custom_call_target="tpu_custom_call" | custom-call | flops 3623878656 | bytes 7077888 | tf_op jit(solution)/shard_map/pallas_call | solution.py:493
  77.9 3.0 %shard_map.56 = f32[64,12288]{1,0:T(8,128)} custom-call(s16[3,16,64,256]{3,2,1,0:T(8,128)(2,1)} %get-tuple-element.7.codes_ref, f32[2,64,128]{2,1,0:T(8,128)} %get-tuple-element.8.terms_ref), custom_call_target="tpu_custom_call" | custom-call | tf_op jit(solution)/shard_map/pallas_call | solution.py:537

commit v4 on v3

--- a/solution.py
+++ b/solution.py
@@ -33,6 +33,7 @@
     picks,
     gain,
     head,
+    turned,
     cnt,
     gains,
     squares,
@@ -147,6 +148,34 @@
     one_hot = (iota((hidden.shape[1], slots), 0) == picks[...]).astype(jnp.bfloat16)
     selected = jnp.dot(hidden[...], one_hot, preferred_element_type=jnp.float32).astype(jnp.bfloat16)
 
+    turn = 256 if width % 256 == 0 else width // 3
+
+    def turn_some(i, c):
+        at = pl.ds(pl.multiple_of(i * turn, turn), turn)
+        turned[at, :] = head[:, at].T
+        return c
+
+    loads[3].wait()
+    thirds = [width // turn * i // 3 for i in range(4)]
+    lax.fori_loop(thirds[0], thirds[1], turn_some, 0)
+
+    cnt_received()
+    group = iota((n_seq, 8, 128), 0)
+    every = cnt[...]
+    offset = jnp.sum(jnp.where(group < s, every, 0), axis=0)[0:1, 0:1]
+    count = jnp.sum(jnp.where(group == s, every, 0), axis=0)[0:1, 0:1]
+
+    slot = iota((total, slots), 1)
+    placing = ((iota((total, slots), 0) == offset + slot) & (slot < count)).astype(jnp.bfloat16)
+
+    compact = lax.dot_general(
+        placing, selected, (((1,), (1,)), ((), ())), preferred_element_type=jnp.float32
+    ).astype(jnp.bfloat16)
+    place[...] = compact.reshape(n_seq, rows, features)
+    plc_start, plc_received, plc_sent = exchange(
+        "seq", seq_peers, lambda peer: place.at[peer], placed.at[s], placed.at[pl.ds(0, n_seq - 1)], plc_sem
+    )
+    plc_start()
     loads[2].wait()
     line = gain[...].reshape(1, features)
     line = jnp.concatenate([line, jnp.zeros((1, -features % 128), jnp.float32)], axis=1)
@@ -158,34 +187,10 @@
     )
     gain_start()
 
-    cnt_received()
-    group = iota((n_seq, 8, 128), 0)
-    every = cnt[...]
-    offset = jnp.sum(jnp.where(group < s, every, 0), axis=0)[0:1, 0:1]
-    count = jnp.sum(jnp.where(group == s, every, 0), axis=0)[0:1, 0:1]
-
-    slot = iota((total, slots), 1)
-    placing = ((iota((total, slots), 0) == offset + slot) & (slot < count)).astype(jnp.bfloat16)
-
-    compact = lax.dot_general(
-        placing, selected, (((1,), (1,)), ((), ())), preferred_element_type=jnp.float32
-    ).astype(jnp.bfloat16)
-    place[...] = compact.reshape(n_seq, rows, features)
-    plc_start, plc_received, plc_sent = exchange(
-        "seq", seq_peers, lambda peer: place.at[peer], placed.at[s], placed.at[pl.ds(0, n_seq - 1)], plc_sem
-    )
-    plc_start()
+    lax.fori_loop(thirds[1], thirds[2], turn_some, 0)
     placed[pl.ds(s, 1)] = place[pl.ds(s, 1)]
     plc_received()
     block = jnp.sum(placed[...].astype(jnp.float32), axis=0).astype(jnp.bfloat16)
-
-    wide = block.astype(jnp.float32)
-    row_eye = iota((rows, 128), 0) == iota((rows, 128), 1)
-    square = jnp.sum(jnp.where(row_eye, jnp.sum(wide * wide, axis=1, keepdims=True), 0.0), axis=0, keepdims=True)
-    squares[pl.ds(v, 1)] = jnp.broadcast_to(square, (8, 128))[None]
-    sqs_start, sqs_received, sqs_sent = exchange(
-        "vocab", vocab_peers, lambda peer: squares.at[v], squares.at[v], squares.at[pl.ds(0, n_vocab - 1)], sqs_sem
-    )
 
     part_of = z // (n_z // 2)
     kept = core == part_of
@@ -209,7 +214,7 @@
     def _():
         along(0, block_out, feats.at[mine]).start()
 
-    sqs_start()
+    lax.fori_loop(thirds[2], thirds[3], turn_some, 0)
 
     @pl.when(kept)
     def _():
@@ -220,14 +225,23 @@
     def _():
         along(1, feats, feats).wait_recv()
 
+    raw = jnp.concatenate([feats[i] for i in range(n_z)], axis=1).astype(jnp.float32)
+
+    row_eye = iota((rows, 128), 0) == iota((rows, 128), 1)
+    square = jnp.sum(jnp.where(row_eye, jnp.sum(raw * raw, axis=1, keepdims=True), 0.0), axis=0, keepdims=True)
+    squares[pl.ds(core, 1)] = jnp.broadcast_to(square, (8, 128))[None]
+    tell_squares = pltpu.make_async_remote_copy(
+        src_ref=squares.at[core], dst_ref=squares.at[core], send_sem=sqs_sem.at[0], recv_sem=sqs_sem.at[1],
+        device_id={"vocab": sibling}, device_id_type=MESH,
+    )
+    tell_squares.start()
     gain_received()
-    sqs_received()
-    raw = jnp.concatenate([feats[i] for i in range(n_z)], axis=1).astype(jnp.float32)
     held = gains[pl.ds(core * n_z, n_z)]
     scale = jnp.concatenate(
         [held[i, c // 128 : c // 128 + 1, : min(128, features - c)] for i in range(n_z) for c in range(0, features, 128)],
         axis=1,
     )
+    tell_squares.wait_recv()
     mean_square = jnp.sum(squares[...], axis=0)[0:1] / width
     mean_square = jnp.sum(jnp.where(row_eye, mean_square, 0.0), axis=1, keepdims=True)
     own = (raw * lax.rsqrt(mean_square + EPSILON) * scale).astype(jnp.bfloat16)
@@ -276,7 +290,6 @@
                 second(order, j, p).start()
             over(core, order, j, 0).start()
 
-    loads[3].wait()
     level[pl.ds(total, slots)] = jnp.zeros((slots, entries), jnp.int32)
     rounds = entries // COLUMNS
 
@@ -289,8 +302,8 @@
         at = pl.ds(pl.multiple_of(i * COLUMNS, COLUMNS), COLUMNS)
         return at, lax.dot_general(
             rows_x[j, k].reshape(block_rows, half_width),
-            head[at, pl.ds(pl.multiple_of(k * half_width, half_width), half_width)],
-            (((1,), (1,)), ((), ())),
+            turned[pl.ds(pl.multiple_of(k * half_width, half_width), half_width), at],
+            (((1,), (0,)), ((), ())),
             preferred_element_type=jnp.float32,
         )
 
@@ -418,7 +431,7 @@
     cnt_sent()
     gain_sent()
     plc_sent()
-    sqs_sent()
+    tell_squares.wait_send()
 
     @pl.when(kept)
     def _():
@@ -503,9 +516,10 @@
                 pltpu.VMEM((1, slots), jnp.int32),
                 pltpu.VMEM((features,), jnp.float32),
                 pltpu.VMEM((entries, width), jnp.bfloat16),
+                pltpu.VMEM((width, entries), jnp.bfloat16),
                 pltpu.VMEM((n_seq, 8, 128), jnp.int32),
                 pltpu.VMEM((n_vocab, 8, 128), jnp.float32),
-                pltpu.VMEM((n_vocab, 8, 128), jnp.float32),
+                pltpu.VMEM((2, 8, 128), jnp.float32),
                 pltpu.VMEM((n_seq, rows, features), jnp.bfloat16),
                 pltpu.VMEM((n_seq, rows, features), jnp.bfloat16),
                 pltpu.VMEM((rows, features), jnp.bfloat16),

time: 81 us -> 77.9 us (0.962)
  Pallas kernels: 80.3 us -> 77.1 us
    pallas_call x1, Pallas kernels: 77.2 us -> 74.1 us  [local(): pl.pallas_call(functools.partial(kernel, (n_seq, n_vocab, side, slots, to...]
where the time goes in v4:
time: 77.9 us; the launch traced here: 77.8 us
  Pallas kernels  77.1 us (99%)
    pallas_call x1, Pallas kernels, local(): pl.pallas_call(functools.partial(kernel, (n_seq, n_vocab, side, slots, to...  74.1 us
    pallas_call x1, Pallas kernels, local(): pl.pallas_call(decode, out_shape=jax.ShapeDtypeStruct((slots, n_seq * ent...  3.03 us

profile of v4, /device:TPU:1, one launch (start us, length us, event | category | flops | bytes accessed | tf_op | source)
XLA Modules:
  0.0 77.8 jit_solution(14022697025314528950)
XLA Ops:
  0.7 74.1 %shard_map.55 = (s16[3,16,64,256]{3,2,1,0:T(8,128)(2,1)}, f32[2,64,128]{2,1,0:T(8,128)}) custom-call(bf16[288,2048]{1,0:T(8,128)(2,1)} %bitcast.3, s32[1,64]{1,0:T(1,128)} %picks_ref.1, s32[1]{0:T(128)S(6)} %copy.6.counts_ref, f32[288]{0:T(512)} %gain_ref.1, bf16[768,4608]{1,0:T(8,128)(2,1)} %head_ref.1), custom_call_target="tpu_custom_call" | custom-call | flops 3623878656 | bytes 7077888 | tf_op jit(solution)/shard_map/pallas_call | solution.py:506
  74.7 3.0 %shard_map.56 = f32[64,12288]{1,0:T(8,128)} custom-call(s16[3,16,64,256]{3,2,1,0:T(8,128)(2,1)} %get-tuple-element.7.codes_ref, f32[2,64,128]{2,1,0:T(8,128)} %get-tuple-element.8.terms_ref), custom_call_target="tpu_custom_call" | custom-call | tf_op jit(solution)/shard_map/pallas_call | solution.py:551

commit v5 on v4

--- a/solution.py
+++ b/solution.py
@@ -253,24 +253,30 @@
             return ((x + p) % side) * side + y
         return x * side + (y + p) % side
 
+    def hop(src, dst, sems, j, order, p):
+        return pltpu.make_async_remote_copy(
+            src_ref=src, dst_ref=dst, send_sem=sems[0].at[j], recv_sem=sems[1].at[j],
+            device_id={"seq": across(order, p)}, device_id_type=MESH,
+        )
+
     def first(order, j):
+        return hop(rows_x.at[0, core, order, 0], rows_x.at[j, core, order, 0], (one_s, one_r), j, order, j)
+
+    def first_both(j):
+        many = rows_x.at[j, core, :, 0]
+        return hop(many, many, (one_s, one_r), j, 0, j)
+
+    def second(order, j, p):
+        return hop(rows_x.at[j, core, order, 0], rows_x.at[j, core, order, p], (two_s, two_r), j, 1 - order, p)
+
+    def second_all(j):
+        many = rows_x.at[j, core, :, pl.ds(1, side - 1)]
+        return hop(many, many, (two_s, two_r), j, 0, 1)
+
+    def over(kind, j):
+        at = rows_x.at[j, kind]
         return pltpu.make_async_remote_copy(
-            src_ref=rows_x.at[0, core, order, 0], dst_ref=rows_x.at[j, core, order, 0],
-            send_sem=one_s.at[order, j], recv_sem=one_r.at[order, j],
-            device_id={"seq": across(order, j)}, device_id_type=MESH,
-        )
-
-    def second(order, j, p):
-        return pltpu.make_async_remote_copy(
-            src_ref=rows_x.at[j, core, order, 0], dst_ref=rows_x.at[j, core, order, p],
-            send_sem=two_s.at[order, j, p], recv_sem=two_r.at[order, j, p],
-            device_id={"seq": across(1 - order, p)}, device_id_type=MESH,
-        )
-
-    def over(kind, order, j, p):
-        at = rows_x.at[j, kind, order, p]
-        return pltpu.make_async_remote_copy(
-            src_ref=at, dst_ref=at, send_sem=fwd_s.at[order, j, p], recv_sem=fwd_r.at[order, j, p],
+            src_ref=at, dst_ref=at, send_sem=fwd_s.at[j], recv_sem=fwd_r.at[j],
             device_id={"vocab": sibling}, device_id_type=MESH,
         )
 
@@ -281,14 +287,14 @@
     for p in near:
         for order in range(2):
             second(order, 0, p).start()
-    for order in range(2):
-        over(core, order, 0, 0).start()
-    for j in near:
-        for order in range(2):
-            first(order, j).wait_recv()
-            for p in near:
+    def spread(j):
+        first_both(j).wait_recv()
+        for p in near:
+            for order in range(2):
                 second(order, j, p).start()
-            over(core, order, j, 0).start()
+
+    for j in near[:-1]:
+        spread(j)
 
     level[pl.ds(total, slots)] = jnp.zeros((slots, entries), jnp.int32)
     rounds = entries // COLUMNS
@@ -385,14 +391,12 @@
                 expo[pl.ds(pl.multiple_of(row_of(order, j, p), HALF), HALF)] = summed[low : low + HALF]
 
     for j in [0] + near:
-        for p in near:
-            for order in range(2):
-                second(order, j, p).wait_recv()
-                over(core, order, j, p).start()
+        second_all(j).wait_recv()
+        over(core, j).start()
+        if j == 0:
+            spread(last)
         begin_block(j)
-        for p in [0] + near:
-            for order in range(2):
-                over(1 - core, order, j, p).wait_recv()
+        over(1 - core, j).wait_recv()
         end_block(j)
 
     square_eye = iota((128, 128), 0) == iota((128, 128), 1)
@@ -442,15 +446,11 @@
     def _():
         along(1, feats, feats).wait_send()
 
-    for order in range(2):
-        over(core, order, 0, 0).wait_send()
-        for j in near:
-            first(order, j).wait_send()
-            over(core, order, j, 0).wait_send()
-        for j in [0] + near:
-            for p in near:
-                second(order, j, p).wait_send()
-                over(core, order, j, p).wait_send()
+    for j in near:
+        first_both(j).wait_send()
+    for j in [0] + near:
+        second_all(j).wait_send()
+        over(core, j).wait_send()
     sma_sent()
     smb_sent()
     write_terms.wait()
@@ -537,9 +537,9 @@
                 pltpu.SemaphoreType.DMA((entries // COLUMNS,)),
                 *[pltpu.SemaphoreType.DMA((2,))] * 7,
                 *dma(entries // COLUMNS),
-                *dma(2, side),
-                *dma(2, side, side),
-                *dma(2, side, side),
+                *dma(side),
+                *dma(side),
+                *dma(side),
             ],
             compiler_params=pltpu.CompilerParams(
                 collective_id=0, has_side_effects=True, vmem_limit_bytes=VMEM_BYTES

time: 77.9 us -> 77.9 us (level)
  no operation moved by 1% of the time
where the time goes in v5:
time: 77.9 us; the launch traced here: 77.7 us
  Pallas kernels  77.1 us (99%)
    pallas_call x1, Pallas kernels, local(): pl.pallas_call(functools.partial(kernel, (n_seq, n_vocab, side, slots, to...  74.1 us
    pallas_call x1, Pallas kernels, local(): pl.pallas_call(decode, out_shape=jax.ShapeDtypeStruct((slots, n_seq * ent...  3.03 us

profile of v5, /device:TPU:1, one launch (start us, length us, event | category | flops | bytes accessed | tf_op | source)
XLA Modules:
  0.0 77.7 jit_solution(11342961835966716414)
XLA Ops:
  0.7 74.1 %shard_map.55 = (s16[3,16,64,256]{3,2,1,0:T(8,128)(2,1)}, f32[2,64,128]{2,1,0:T(8,128)}) custom-call(bf16[288,2048]{1,0:T(8,128)(2,1)} %bitcast.3, s32[1,64]{1,0:T(1,128)} %picks_ref.1, s32[1]{0:T(128)S(6)} %copy.6.counts_ref, f32[288]{0:T(512)} %gain_ref.1, bf16[768,4608]{1,0:T(8,128)(2,1)} %head_ref.1), custom_call_target="tpu_custom_call" | custom-call | flops 3623878656 | bytes 7077888 | tf_op jit(solution)/shard_map/pallas_call | solution.py:506
  74.7 3.0 %shard_map.56 = f32[64,12288]{1,0:T(8,128)} custom-call(s16[3,16,64,256]{3,2,1,0:T(8,128)(2,1)} %get-tuple-element.7.codes_ref, f32[2,64,128]{2,1,0:T(8,128)} %get-tuple-element.8.terms_ref), custom_call_target="tpu_custom_call" | custom-call | tf_op jit(solution)/shard_map/pallas_call | solution.py:551
